TPU v7x, 32 devices: a whole 2x2x4 slice. The times are simulated.
32 devices in a mesh: groups: 2 (over y), row: 4 (over x, core), col: 4 (over z).
Axes of the slice: x: 2, y: 2, z: 4, core: 2. Of those that a mesh axis runs over, the one named last changes fastest.
Arguments:
- pair: bfloat16 [1024, 512, 128], P(('groups', 'row'), 'col'), parts along dimension 0, may hold values from -6 to 6
- token_mask: int32 [1024], P('groups'), parts along dimension 0, may hold values 0 or 1
- token_count: int32 [2], P('groups'), parts along dimension 0, may hold values from 256 to 512
- out_inputs: bfloat16 [128, 512], replicated, may hold values from -0.5 to 0.5
- out_gating: bfloat16 [128, 128], replicated, may hold values from -0.5 to 0.5
- out_final: bfloat16 [128, 128], replicated, may hold values from -0.5 to 0.5
- in_inputs: bfloat16 [128, 512], replicated, may hold values from -0.5 to 0.5
- in_gating: bfloat16 [128, 128], replicated, may hold values from -0.5 to 0.5
- in_final: bfloat16 [128, 128], replicated, may hold values from -0.5 to 0.5
Outputs:
- updated: bfloat16 [1024, 512, 128], P(('groups', 'row'), 'col'), parts along dimension 0
There are 2 independent parts, one for each index of `groups`. A program takes and returns all parts, laid end to end along the dimension named above; an argument that names none is the same for every part. Nothing has to cross between parts.
Inputs may be any that keep to these rules, and one draw needn't show every extreme that they name: Token positions token_count and beyond are padding.
All inputs are finite; a program needn't handle non-finite values.
Results may differ from a plain program's by a relative error of at most 0.0054.
Values may be sent and summed in bfloat16 or wider, within the bound.
A program may use at most 192 MiB of HBM per device.

v0:
```python
import jax
import jax.numpy as jnp
from jax import lax
from jax.sharding import PartitionSpec as P


def spread(array, axis, root):
    mine = lax.axis_index(axis) == root
    return lax.psum(jnp.where(mine, array, jnp.zeros_like(array)), axis)


def layer_norm(x):
    mean = jnp.mean(x, axis=-1, keepdims=True)
    centred = x - mean
    var = jnp.mean(centred * centred, axis=-1, keepdims=True)
    return centred * lax.rsqrt(var + 1e-05)


def prepare(field, pmask, w_inputs, w_gating):
    hidden = w_inputs.shape[1] // 4
    normed = layer_norm(field.astype(jnp.float32)).astype(jnp.bfloat16)
    flat = normed.reshape(-1, normed.shape[-1])
    proj = jnp.dot(flat, w_inputs, preferred_element_type=jnp.float32)
    proj = proj.reshape(field.shape[0], field.shape[1], 4 * hidden)
    left = (
        pmask[..., None] * jax.nn.sigmoid(proj[..., :hidden]) * proj[..., hidden : 2 * hidden]
    ).astype(jnp.bfloat16)
    right = (
        pmask[..., None]
        * jax.nn.sigmoid(proj[..., 2 * hidden : 3 * hidden])
        * proj[..., 3 * hidden :]
    ).astype(jnp.bfloat16)
    gate = jax.nn.sigmoid(jnp.dot(flat, w_gating, preferred_element_type=jnp.float32))
    return (left, right, gate.reshape(field.shape[0], field.shape[1], -1))


def finish(field, tri, gate, w_final):
    tnorm = layer_norm(tri).astype(jnp.bfloat16)
    flat = tnorm.reshape(-1, tnorm.shape[-1])
    value = jnp.dot(flat, w_final, preferred_element_type=jnp.float32).reshape(gate.shape)
    return (field.astype(jnp.float32) + gate * value).astype(jnp.bfloat16)


def local(
    pair, token_mask, token_count, out_inputs, out_gating, out_final, in_inputs, in_gating, in_final
):
    rows = pair.shape[0]
    cols = pair.shape[1]
    row_index = lax.axis_index("row")
    col_index = lax.axis_index("col")
    ratio = lax.axis_size("col") // lax.axis_size("row")
    positions = lax.iota(jnp.int32, token_mask.shape[0])
    valid = token_mask * (positions < token_count[0]).astype(jnp.int32)
    validf = valid.astype(jnp.float32)
    row_valid = lax.dynamic_slice_in_dim(validf, row_index * rows, rows)
    col_valid = lax.dynamic_slice_in_dim(validf, col_index * cols, cols)
    pmask = row_valid[:, None] * col_valid[None, :]
    left, right, gate = prepare(pair, pmask, out_inputs, out_gating)
    right_rows = lax.all_gather(right, "col", axis=1, tiled=True)
    portion = lax.dynamic_slice_in_dim(right_rows, col_index % ratio * cols, cols, 0)
    right_mine = spread(portion, "row", col_index // ratio)
    matching = right_mine
    tri = jnp.einsum(
        "ikh,jkh->ijh",
        lax.all_gather(left, "col", axis=1, tiled=True),
        matching,
        preferred_element_type=jnp.float32,
    )
    middle = finish(pair, tri, gate, out_final)
    left, right, gate = prepare(middle, pmask, in_inputs, in_gating)
    left_cols = lax.all_gather(left, "row", axis=0, tiled=True)
    owned = []
    for member in range(ratio):
        owned.append(spread(left_cols, "col", row_index * ratio + member))
    left_mine = jnp.concatenate(owned, axis=1)
    matching = left_mine
    tri = jnp.einsum(
        "kih,kjh->ijh",
        matching,
        lax.all_gather(right, "row", axis=0, tiled=True),
        preferred_element_type=jnp.float32,
    )
    return finish(middle, tri, gate, in_final)


def solution(mesh):
    in_specs = (
        P(("groups", "row"), "col", None),
        P("groups"),
        P("groups"),
        P(),
        P(),
        P(),
        P(),
        P(),
        P(),
    )
    out_specs = P(("groups", "row"), "col", None)
    return jax.shard_map(local, mesh=mesh, in_specs=in_specs, out_specs=out_specs, check_vma=False)
```

profile of v0, /device:TPU:0, one launch (start us, length us, event | category | flops | bytes accessed | tf_op | source)
XLA Modules:
  0.0 1854.4 jit_solution(11469661870407682885)
XLA Ops:
  11.2 6.0 fusion.12
  17.2 6.2 fusion.13
  23.6 15.4 fusion.38
  39.1 15.5 fusion.26
  55.4 288.8 %all-gather.5.cloned.1.call-done = bf16[128,512,128]{2,1,0:T(8,128)(2,1)} async-done(((bf16[128,128,128]{2,1,0:T(8,128)(2,1)}), bf16[128,512,128]{2,1,0:T(8,128)(2,1)}) %all-gather.5.cloned.1.call-update) | async-done | bytes 16777232 | tf_op jit(solution)/shard_map/all_gather | solution.py:59
  344.2 14.3 broadcast_select_fusion.1
  359.3 8.2 fusion.5
  367.5 263.3 %all-gather.7.cloned.1.call-done = bf16[128,512,128]{2,1,0:T(8,128)(2,1)} async-done(((bf16[128,128,128]{2,1,0:T(8,128)(2,1)}), bf16[128,512,128]{2,1,0:T(8,128)(2,1)}) %all-gather.7.cloned.1.call-update) | async-done | bytes 16777232 | tf_op jit(solution)/shard_map/all_gather | solution.py:65
  630.8 23.5 %copy.31 = bf16[128,512,128]{1,0,2:T(8,128)(2,1)} copy(bf16[128,512,128]{2,1,0:T(8,128)(2,1)} %all-gather.7.cloned.1.call-done) | data formatting | bytes 33554432 | tf_op jit(solution)/shard_map/all_gather | solution.py:65
  654.3 265.5 %all-reduce.3.cloned.1.call-done = bf16[128,512,128]{2,1,0:T(8,128)(2,1)} async-done(((bf16[128,512,128]{2,1,0:T(8,128)(2,1)}), bf16[128,512,128]{2,1,0:T(8,128)(2,1)}) %all-reduce.3.cloned.1.call-update) | async-done | bytes 16777232 | tf_op jit(solution)/shard_map/psum | solution.py:9
  919.8 23.9 %copy.30 = bf16[128,512,128]{1,0,2:T(8,128)(2,1)} copy(bf16[128,512,128]{2,1,0:T(8,128)(2,1)} %all-reduce.3.cloned.1.call-done) | data formatting | bytes 33554432 | tf_op jit(solution)/shard_map/psum | solution.py:9
  943.7 16.4 bitcast_reduce_fusion.1
  960.3 4.3 multiply_reduce_fusion.1
  964.8 6.7 multiply_convert_fusion.1
  971.5 7.3 copy.36
  978.7 8.2 convert_reduce_fusion
  987.0 4.8 fusion.10
  991.8 4.9 fusion.11
  996.7 13.1 fusion.36
  1009.8 15.6 fusion.16
  1026.0 105.5 %all-gather.11.cloned.1.call-done = bf16[512,128,128]{2,1,0:T(8,128)(2,1)} async-done(((bf16[128,128,128]{2,1,0:T(8,128)(2,1)}), bf16[512,128,128]{2,1,0:T(8,128)(2,1)}) %all-gather.11.cloned.1.call-update) | async-done | bytes 16777232 | tf_op jit(solution)/shard_map/all_gather | solution.py:71
  1131.5 23.3 %copy.37 = bf16[512,128,128]{1,0,2:T(8,128)(2,1)} copy(bf16[512,128,128]{2,1,0:T(8,128)(2,1)} %all-gather.11.cloned.1.call-done) | data formatting | bytes 33554432 | tf_op jit(solution)/shard_map/all_gather | solution.py:71
  1154.8 13.8 broadcast_select_fusion
  1169.3 7.9 fusion.4
  1177.2 61.6 %all-gather.9.cloned.1.call-done = bf16[512,128,128]{2,1,0:T(8,128)(2,1)} async-done(((bf16[128,128,128]{2,1,0:T(8,128)(2,1)}), bf16[512,128,128]{2,1,0:T(8,128)(2,1)}) %all-gather.9.cloned.1.call-update) | async-done | bytes 16777232 | tf_op jit(solution)/shard_map/all_gather | solution.py:80
  1238.9 26.0 %copy.38 = bf16[512,128,128]{0,1,2:T(8,128)(2,1)} copy(bf16[512,128,128]{2,1,0:T(8,128)(2,1)} %all-gather.9.cloned.1.call-done) | data formatting | bytes 33554432 | tf_op jit(solution)/shard_map/all_gather | solution.py:80
  1264.9 538.5 %all-reduce.5.cloned.1.call-done = bf16[512,128,128]{1,0,2:T(8,128)(2,1)} async-done(((bf16[512,128,128]{1,0,2:T(8,128)(2,1)}), bf16[512,128,128]{1,0,2:T(8,128)(2,1)}) %all-reduce.5.cloned.1.call-update) | async-done | bytes 16777232 | tf_op jit(solution)/shard_map/psum | solution.py:9
  1803.4 16.4 bitcast_reduce_fusion
  1820.0 4.3 multiply_reduce_fusion
  1824.5 6.6 multiply_convert_fusion
  1831.2 7.3 copy.43
  1838.4 9.1 fusion.15
  (54 shorter events, 7.7 us)
Async XLA Ops:
  6.5 17.1 copy-start
  6.5 337.7 %all-gather.5.cloned.1.call-start = ((), (), s32[]{:S(2)}) async-start(), calls=%async_computation | async-start | bytes 20971520 | tf_op jit(solution)/shard_map/all_gather | solution.py:59
  6.5 10.6 copy-start.3
  7.3 16.1 copy-start.8
  54.6 576.2 %all-gather.7.cloned.1.call-start = ((), (), s32[]{:S(2)}) async-start(), calls=%async_computation.2 | async-start | bytes 20971520 | tf_op jit(solution)/shard_map/all_gather | solution.py:65
  55.3 864.5 %all-reduce.3.cloned.1.call-start = ((), (), s32[]{:S(2)}) async-start(), calls=%async_computation.1 | async-start | bytes 33554432 | tf_op jit(solution)/shard_map/psum | solution.py:9
  358.6 0.8 copy-start.9
  358.6 772.9 %all-gather.11.cloned.1.call-start = ((), (), s32[]{:S(2)}) async-start(), calls=%async_computation.4 | async-start | bytes 20971520 | tf_op jit(solution)/shard_map/all_gather | solution.py:71
  964.8 14.0 copy-start.6
  986.9 22.9 %copy-start.2 = (bf16[128,128,128]{2,1,0:T(8,128)(2,1)}, bf16[128,128,128]{2,1,0:T(8,128)(2,1)S(1)}, u32[]{:S(2)}) copy-start(bf16[128,128,128]{2,1,0:T(8,128)(2,1)S(1)} %get-tuple-element.14) | copy-start | bytes 12582916
  986.9 9.7 copy-start.5
  996.7 13.1 copy-start.4
  1025.4 213.5 %all-gather.9.cloned.1.call-start = ((), (), s32[]{:S(2)}) async-start(), calls=%async_computation.3 | async-start | bytes 20971520 | tf_op jit(solution)/shard_map/all_gather | solution.py:80
  1026.0 777.4 %all-reduce.5.cloned.1.call-start = ((), (), s32[]{:S(2)}) async-start(), calls=%async_computation.5 | async-start | bytes 33554432 | tf_op jit(solution)/shard_map/psum | solution.py:9
  1168.5 0.8 copy-start.10
  1824.5 13.9 copy-start.7
  1838.4 9.1 copy-start.1
Sparse Core Ops, SparseCore 0:
  54.7 289.4 all-gather.4
  345.8 284.9 all-gather.6
  633.3 286.4 all-reduce.2
  1025.5 105.9 all-gather.10
  1132.9 105.9 all-gather.8
  1241.2 562.1 all-reduce.4
where the time goes:
time: 1860 us; the launch traced here: 1850 us
  waiting for transfers between devices  1520 us (82%)
  local copies, waits for them, and re-layouts  113 us (6%)
  other arithmetic  107 us (6%)
  matrix products  94.7 us (5%)
    psum x2, waiting for transfers between devices, spread(): return lax.psum(jnp.where(mine, array, jnp.zeros_like(array)), axis)  804 us
    all_gather x1, waiting for transfers between devices, local(): right_rows = lax.all_gather(right, 'col', axis=1, tiled=True)  289 us
    all_gather x1, waiting for transfers between devices, local(): lax.all_gather(left, 'col', axis=1, tiled=True)  263 us
    all_gather x1, waiting for transfers between devices, local(): left_cols = lax.all_gather(left, 'row', axis=0, tiled=True)  105 us
    all_gather x1, waiting for transfers between devices, local(): lax.all_gather(right, 'row', axis=0, tiled=True)  61.6 us
  transfers between devices with their start and end apart: 6, of which 6 were waited for; matrix products, arithmetic and copies ran while one was open for 6% of the time, Pallas kernels for 0%

commit v1 on v0

v1 whole, which is shorter than its diff:
```python
import functools

import jax
import jax.numpy as jnp
from jax import lax
from jax.experimental import pallas as pl
from jax.experimental.pallas import tpu as pltpu
from jax.sharding import PartitionSpec as P

AXES = ("row", "col")


def layer_norm(x, axis=-1):
    mean = jnp.mean(x, axis=axis, keepdims=True)
    centred = x - mean
    var = jnp.mean(centred * centred, axis=axis, keepdims=True)
    return centred * lax.rsqrt(var + 1e-05)


def product_kernel(rows, cols, outgoing, a_ref, b_ref, o_ref, a_full, b_full, t_full):
    height, width = a_ref.shape[-2:]
    for r in range(rows):
        for c in range(cols):
            at = (slice(r * height, (r + 1) * height), slice(c * width, (c + 1) * width))
            a_full[at] = a_ref[r * cols + c, 0]
            b_full[at] = b_ref[r * cols + c, 0]
    dims = (((1,), (1,)), ((), ())) if outgoing else (((0,), (0,)), ((), ()))
    t_full[...] = lax.dot_general(
        a_full[...], b_full[...], dims, preferred_element_type=jnp.float32
    ).astype(jnp.bfloat16)
    for r in range(rows):
        for c in range(cols):
            at = (slice(r * height, (r + 1) * height), slice(c * width, (c + 1) * width))
            o_ref[r * cols + c, 0] = t_full[at]


def product(a, b, rows, cols, outgoing):
    parts, hidden, height, width = a.shape
    n = rows * height
    spec = pl.BlockSpec((parts, 1, height, width), lambda h: (0, h, 0, 0))
    return pl.pallas_call(
        functools.partial(product_kernel, rows, cols, outgoing),
        grid=(hidden,),
        in_specs=[spec, spec],
        out_specs=spec,
        out_shape=jax.ShapeDtypeStruct(a.shape, jnp.bfloat16),
        scratch_shapes=[pltpu.VMEM((n, n), jnp.bfloat16)] * 3,
        compiler_params=pltpu.CompilerParams(vmem_limit_bytes=40 * 2**20),
        cost_estimate=pl.CostEstimate(
            flops=2 * hidden * n**3, bytes_accessed=6 * hidden * n * n, transcendentals=0
        ),
    )(a, b)


def exchange(x):
    return lax.all_to_all(x, AXES, 0, 0, tiled=True)


def update(field, pmask, w_inputs, w_gating, w_final, outgoing):
    rows, cols = lax.axis_size("row"), lax.axis_size("col")
    parts = rows * cols
    height, width = field.shape[:2]
    hidden = w_inputs.shape[1] // 4
    normed = layer_norm(field.astype(jnp.float32)).astype(jnp.bfloat16)

    def side(first):
        def one(start):
            w = w_inputs[:, start : start + hidden]
            return lax.dot_general(
                w, normed, (((0,), (2,)), ((), ())), preferred_element_type=jnp.float32
            )

        value = pmask[None] * jax.nn.sigmoid(one(first)) * one(first + hidden)
        return exchange(value.astype(jnp.bfloat16)).reshape(parts, -1, height, width)

    a = side(0)
    b = side(2 * hidden)
    gate = jax.nn.sigmoid(jnp.dot(normed, w_gating, preferred_element_type=jnp.float32))
    tri = product(a, b, rows, cols, outgoing)
    tri = exchange(tri.reshape(hidden, height, width)).astype(jnp.float32)
    tnorm = layer_norm(tri, 0).astype(jnp.bfloat16)
    value = lax.dot_general(
        tnorm, w_final, (((0,), (0,)), ((), ())), preferred_element_type=jnp.float32
    )
    return (field.astype(jnp.float32) + gate * value).astype(jnp.bfloat16)


def local(
    pair, token_mask, token_count, out_inputs, out_gating, out_final, in_inputs, in_gating, in_final
):
    height, width = pair.shape[:2]
    positions = lax.iota(jnp.int32, token_mask.shape[0])
    valid = (token_mask * (positions < token_count[0]).astype(jnp.int32)).astype(jnp.float32)
    row_valid = lax.dynamic_slice_in_dim(valid, lax.axis_index("row") * height, height)
    col_valid = lax.dynamic_slice_in_dim(valid, lax.axis_index("col") * width, width)
    pmask = row_valid[:, None] * col_valid[None, :]
    middle = update(pair, pmask, out_inputs, out_gating, out_final, True)
    return update(middle, pmask, in_inputs, in_gating, in_final, False)


def solution(mesh):
    tile = P(("groups", "row"), "col", None)
    in_specs = (tile, P("groups"), P("groups")) + (P(),) * 6
    return jax.shard_map(local, mesh=mesh, in_specs=in_specs, out_specs=tile, check_vma=False)
```

time: 1860 us -> 684 us (0.37)
  waiting for transfers between devices: 1520 us -> 165 us
  blocking collectives: 0 us -> 392 us
  other arithmetic: 107 us -> 16 us
  local copies, waits for them, and re-layouts: 113 us -> 31.6 us
  matrix products: 94.7 us -> 42.3 us
    psum x2 -> x0, waiting for transfers between devices: 804 us -> none  [spread(): return lax.psum(jnp.where(mine, array, jnp.zeros_like(array)), axis)]
    all_gather x4 -> x0, waiting for transfers between devices: 719 us -> none  [the longest x1 289 us: local(): right_rows = lax.all_gather(right, 'col', axis=1, tiled=True)]
    all_to_all x0 -> x4, blocking collectives: none -> 392 us  [exchange(): return lax.all_to_all(x, AXES, 0, 0, tiled=True)]
    all_to_all x0 -> x2, waiting for transfers between devices: none -> 165 us  [exchange(): return lax.all_to_all(x, AXES, 0, 0, tiled=True)]
    all_gather x3 -> x0, local copies, waits for them, and re-layouts: 72.9 us -> none  [the longest x1 26 us: local(): lax.all_gather(right, 'row', axis=0, tiled=True)]
    dot_general x8 -> x12, matrix products: 94.7 us -> 42.3 us  [the longest x8 26.5 us: one(): lax.dot_general(w, normed, (((0,), (2,)), ((), ())), preferred_element_ty...]
    convert_element_type x7 -> x3, other arithmetic: 55.6 us -> 3.2 us  [the longest x2 3.19 us: update(): tnorm = layer_norm(tri, 0).astype(jnp.bfloat16)]
    select_n x2 -> x0, other arithmetic: 28.1 us -> none  [spread(): return lax.psum(jnp.where(mine, array, jnp.zeros_like(array)), axis)]
  transfers between devices with their start and end apart: 6 -> 2, of which waited for: 6 -> 2; matrix products, arithmetic and copies ran while one was open for 6% -> 4% of each run, Pallas kernels for 0% -> 0%
where the time goes in v1:
time: 684 us; the launch traced here: 675 us
  blocking collectives  392 us (57%)
  waiting for transfers between devices  165 us (24%)
  matrix products  42.3 us (6%)
  local copies, waits for them, and re-layouts  31.6 us (5%)
  other arithmetic  16 us (2%)
  Pallas kernels  15.1 us (2%)
  starting transfers between devices  12.2 us (2%)
    all_to_all x4, blocking collectives, exchange(): return lax.all_to_all(x, AXES, 0, 0, tiled=True)  392 us
    all_to_all x2, waiting for transfers between devices, exchange(): return lax.all_to_all(x, AXES, 0, 0, tiled=True)  165 us
    dot_general x8, matrix products, one(): lax.dot_general(w, normed, (((0,), (2,)), ((), ())), preferred_element_ty...  26.5 us
    convert_element_type x4, local copies, waits for them, and re-layouts, side(): value.astype(jnp.bfloat16)  18.7 us
    pallas_call x2, Pallas kernels, product(): pl.pallas_call(functools.partial(product_kernel, rows, cols, outgoing), g...  15.1 us
  transfers between devices with their start and end apart: 2, of which 2 were waited for; matrix products, arithmetic and copies ran while one was open for 4% of the time, Pallas kernels for 0%

profile of v1, /device:TPU:0, one launch (start us, length us, event | category | flops | bytes accessed | tf_op | source)
XLA Modules:
  0.0 675.5 jit_solution(5083064954407974913)
XLA Ops:
  0.7 6.4 copy.40
  7.1 3.4 convert_reduce_fusion.1
  10.5 3.9 fusion.10
  14.7 3.7 fusion.39
  18.3 3.5 fusion.22
  21.9 4.7 copy.47
  26.5 7.6 %all-to-all-start = ((bf16[128,128,128]{2,1,0:T(8,128)(2,1)}), bf16[128,128,128]{2,1,0:T(8,128)(2,1)}, u32[]{:S(2)}, u32[]{:S(2)}) async-start(bf16[128,128,128]{2,1,0:T(8,128)(2,1)} %copy.47), calls=%async_computation | async-start | bytes 8388608 | tf_op jit(solution)/shard_map/all_to_all | solution.py:56
  34.2 3.7 fusion.36
  37.8 3.5 fusion.23
  41.4 4.7 copy.52
  46.1 82.5 %all-to-all-done = bf16[128,128,128]{2,1,0:T(8,128)(2,1)} async-done(((bf16[128,128,128]{2,1,0:T(8,128)(2,1)}), bf16[128,128,128]{2,1,0:T(8,128)(2,1)}, u32[]{:S(2)}, u32[]{:S(2)}) %all-to-all-start) | async-done | bytes 4194336 | tf_op jit(solution)/shard_map/all_to_all | solution.py:56
  128.6 98.2 %all_to_all.30 = bf16[128,128,128]{2,1,0:T(8,128)(2,1)S(1)} all-to-all(bf16[128,128,128]{2,1,0:T(8,128)(2,1)} %copy.52), channel_id=1, replica_groups=mesh['groups'=2,'row'=4,'col'=4] {'row','col'}, dimensions={0} | all-to-all | bytes 8388608 | tf_op jit(solution)/shard_map/all_to_all | solution.py:56
  226.8 7.4 %shard_map.91 = bf16[16,8,128,128]{3,2,1,0:T(8,128)(2,1)S(1)} custom-call(bf16[16,8,128,128]{3,2,1,0:T(8,128)(2,1)} %bitcast.5.a_ref, bf16[16,8,128,128]{3,2,1,0:T(8,128)(2,1)S(1)} %bitcast.54), custom_call_target="tpu_custom_call" | custom-call | flops 2147483648 | bytes 12582912 | tf_op jit(solution)/shard_map/pallas_call | solution.py:41
  234.2 98.0 %all_to_all.31 = bf16[128,128,128]{2,1,0:T(8,128)(2,1)S(1)} all-to-all(bf16[128,128,128]{2,1,0:T(8,128)(2,1)S(1)} %bitcast.55), channel_id=1, replica_groups=mesh['groups'=2,'row'=4,'col'=4] {'row','col'}, dimensions={0} | all-to-all | bytes 8388608 | tf_op jit(solution)/shard_map/all_to_all | solution.py:56
  334.0 1.9 fusion.15
  335.9 3.2 fusion.20
  339.1 4.2 convert_reduce_fusion
  343.4 1.7 fusion.8
  346.5 3.7 fusion.24
  350.2 4.7 copy.61
  354.8 4.5 all-to-all-start.3
  359.4 3.7 fusion.28
  363.1 3.5 fusion.25
  366.6 4.7 copy.66
  371.3 82.5 %all-to-all-done.3 = bf16[128,128,128]{2,1,0:T(8,128)(2,1)} async-done(((bf16[128,128,128]{2,1,0:T(8,128)(2,1)}), bf16[128,128,128]{2,1,0:T(8,128)(2,1)}, u32[]{:S(2)}, u32[]{:S(2)}) %all-to-all-start.3) | async-done | bytes 4194336 | tf_op jit(solution)/shard_map/all_to_all | solution.py:56
  453.8 98.2 %all_to_all.32 = bf16[128,128,128]{2,1,0:T(8,128)(2,1)S(1)} all-to-all(bf16[128,128,128]{2,1,0:T(8,128)(2,1)} %copy.66), channel_id=1, replica_groups=mesh['groups'=2,'row'=4,'col'=4] {'row','col'}, dimensions={0} | all-to-all | bytes 8388608 | tf_op jit(solution)/shard_map/all_to_all | solution.py:56
  551.9 7.6 %shard_map.92 = bf16[16,8,128,128]{3,2,1,0:T(8,128)(2,1)S(1)} custom-call(bf16[16,8,128,128]{3,2,1,0:T(8,128)(2,1)} %bitcast.16.a_ref, bf16[16,8,128,128]{3,2,1,0:T(8,128)(2,1)S(1)} %bitcast.56), custom_call_target="tpu_custom_call" | custom-call | flops 2147483648 | bytes 12582912 | tf_op jit(solution)/shard_map/pallas_call | solution.py:41
  559.6 97.8 %all_to_all.33 = bf16[128,128,128]{2,1,0:T(8,128)(2,1)S(1)} all-to-all(bf16[128,128,128]{2,1,0:T(8,128)(2,1)S(1)} %bitcast.57), channel_id=1, replica_groups=mesh['groups'=2,'row'=4,'col'=4] {'row','col'}, dimensions={0} | all-to-all | bytes 8388608 | tf_op jit(solution)/shard_map/all_to_all | solution.py:56
  659.1 1.3 fusion.13
  660.5 3.2 fusion.18
  663.8 5.1 fusion.17
  668.9 6.4 copy.69
  (43 shorter events, 5.2 us)
Async XLA Ops:
  0.0 339.1 %copy-start = (bf16[128,128]{1,0:T(8,128)(2,1)S(1)}, bf16[128,128]{1,0:T(8,128)(2,1)}, u32[]{:S(2)}) copy-start(bf16[128,128]{1,0:T(8,128)(2,1)} %param.13) | copy-start | bytes 98308
  0.7 13.8 %copy-start.12 = (s32[512]{0:T(512)S(1)}, s32[512]{0:T(512)}, u32[]{:S(2)}) copy-start(s32[512]{0:T(512)} %param.10) | copy-start | bytes 6148
  0.7 14.0 %copy-start.8 = (bf16[128,512]{1,0:T(8,128)(2,1)S(1)}, bf16[128,512]{1,0:T(8,128)(2,1)}, u32[]{:S(2)}) copy-start(bf16[128,512]{1,0:T(8,128)(2,1)} %param.12) | copy-start | bytes 393220
  14.4 3.9 copy-start.2
  26.5 102.1 %all-to-all-start = ((bf16[128,128,128]{2,1,0:T(8,128)(2,1)}), bf16[128,128,128]{2,1,0:T(8,128)(2,1)}, u32[]{:S(2)}, u32[]{:S(2)}) async-start(bf16[128,128,128]{2,1,0:T(8,128)(2,1)} %copy.47), calls=%async_computation | async-start | bytes 8388608 | tf_op jit(solution)/shard_map/all_to_all | solution.py:56
  34.2 3.7 copy-start.3
  332.2 3.7 copy-start.10
  335.9 3.2 copy-start.4
  339.1 6.1 copy-start.9
  343.3 3.1 copy-start.5
  354.8 98.9 %all-to-all-start.3 = ((bf16[128,128,128]{2,1,0:T(8,128)(2,1)}), bf16[128,128,128]{2,1,0:T(8,128)(2,1)}, u32[]{:S(2)}, u32[]{:S(2)}) async-start(bf16[128,128,128]{2,1,0:T(8,128)(2,1)} %copy.61), calls=%async_computation.3 | async-start | bytes 8388608 | tf_op jit(solution)/shard_map/all_to_all | solution.py:56
  359.4 3.7 copy-start.6
  657.3 3.2 copy-start.11
  660.5 3.2 copy-start.7
  660.5 3.2 copy-start.13
  663.7 11.5 %copy-start.1 = (bf16[128,128]{1,0:T(8,128)(2,1)S(1)}, bf16[128,128]{1,0:T(8,128)(2,1)}, u32[]{:S(2)}) copy-start(bf16[128,128]{1,0:T(8,128)(2,1)} %param.13) | copy-start | bytes 98308

commit v2 on v1

v2 whole, which is shorter than its diff:
```python
import functools

import jax
import jax.numpy as jnp
from jax import lax
from jax.experimental import pallas as pl
from jax.experimental.pallas import tpu as pltpu
from jax.sharding import PartitionSpec as P

CHUNKS = 4


def layer_norm(x, axis=-1):
    mean = jnp.mean(x, axis=axis, keepdims=True)
    centred = x - mean
    var = jnp.mean(centred * centred, axis=axis, keepdims=True)
    return centred * lax.rsqrt(var + 1e-05)


MESH = pl.DeviceIdType.MESH


def triangle_kernel(
    outgoing, chunks, rows, half_cols, a_hbm, b_hbm, o_hbm, a_in, b_in, t_out, a_full, b_full,
    a_send, a_recv, b_send, b_recv, t_send, t_recv, own_sem,
):
    members = rows * half_cols
    depth = a_in.shape[3]
    owned = depth * chunks
    height, width = a_in.shape[-2:]
    row, col = lax.axis_index("row"), lax.axis_index("col")
    half = lax.div(col, half_cols)
    mine = row * half_cols + lax.rem(col, half_cols)
    a_flips = 1 if outgoing else 2
    t_flips = 2 if outgoing else 1

    def side_of(flip):
        return half if flip == 0 else 1 - half

    def ahead(off):
        return lax.rem(mine + off, members)

    def behind(off):
        return lax.rem(mine + members - off, members)

    def place(flip, member):
        return {
            "row": lax.div(member, half_cols),
            "col": side_of(flip) * half_cols + lax.rem(member, half_cols),
        }

    def slots(count, flip):
        return side_of(flip) if count == 2 else 0

    def each(flips, body):
        for flip in reversed(range(flips)):
            first = 1 if flip == 0 else 0

            def one(off, carry, flip=flip):
                body(flip, off)
                return carry

            lax.fori_loop(first, members, one, 0)

    def inward(source, landing, send, recv, flips, q, flip, off, slot_side, slot_member):
        target = ahead(off)
        return pltpu.make_async_remote_copy(
            src_ref=source.at[pl.ds(target * owned + q * depth, depth)],
            dst_ref=landing.at[q, slot_side, slot_member],
            send_sem=send.at[q, flip, off],
            recv_sem=recv.at[q, flip, off],
            device_id=place(flip, target),
            device_id_type=MESH,
        )

    def outward(q, flip, off, o_side, o_member):
        target = ahead(off)
        return pltpu.make_async_remote_copy(
            src_ref=t_out.at[q, slots(t_flips, flip), target],
            dst_ref=o_hbm.at[o_side, pl.ds(o_member * owned + q * depth, depth)],
            send_sem=t_send.at[q, flip, off],
            recv_sem=t_recv.at[q, flip, off],
            device_id=place(flip, target),
            device_id_type=MESH,
        )

    operands = (
        (a_hbm, a_in, a_send, a_recv, a_flips),
        (b_hbm, b_in, b_send, b_recv, 1),
    )

    def local_in(which, q):
        source, landing, _, _, flips = operands[which]
        return pltpu.make_async_copy(
            source.at[pl.ds(mine * owned + q * depth, depth)],
            landing.at[q, slots(flips, 0), mine],
            own_sem.at[which, q],
        )

    def local_out(q):
        return pltpu.make_async_copy(
            t_out.at[q, slots(t_flips, 0), mine],
            o_hbm.at[slots(t_flips, 0), pl.ds(mine * owned + q * depth, depth)],
            own_sem.at[2, q],
        )

    def start_in(q):
        for which in range(2):
            source, landing, send, recv, flips = operands[which]
            each(
                flips,
                lambda flip, off: inward(
                    source, landing, send, recv, flips, q, flip, off, slots(flips, 0), mine
                ).start(),
            )
            local_in(which, q).start()

    def wait_in(q):
        for which in range(2):
            source, landing, send, recv, flips = operands[which]
            each(
                flips,
                lambda flip, off: inward(
                    source, landing, send, recv, flips, q, flip, off, slots(flips, flip), behind(off)
                ).wait_recv(),
            )
            local_in(which, q).wait()

    barrier = pltpu.get_barrier_semaphore()
    each(
        2,
        lambda flip, off: pl.semaphore_signal(
            barrier, inc=1, device_id=place(flip, ahead(off)), device_id_type=MESH
        ),
    )
    pl.semaphore_wait(barrier, 2 * members - 1)

    def fill(full, landing, q, channel, flips):
        for side in range(flips):
            for member in range(members):
                r = (member // half_cols) * height
                c = (side * half_cols + member % half_cols) * width
                full[r : r + height, c : c + width] = landing[q, side, member, channel]

    dims = (((1,), (1,)), ((), ())) if outgoing else (((0,), (0,)), ((), ()))

    ready = min(2, chunks)
    for q in range(ready):
        start_in(q)
    for q in range(chunks):
        wait_in(q)

        def multiply(channel, carry, q=q):
            fill(a_full, a_in, q, channel, a_flips)
            fill(b_full, b_in, q, channel, 1)
            tri = lax.dot_general(
                a_full[...], b_full[...], dims, preferred_element_type=jnp.float32
            ).astype(jnp.bfloat16)
            for side in range(t_flips):
                for member in range(members):
                    r = (member // half_cols) * height
                    c = (side * half_cols + member % half_cols) * width
                    t_out[q, side, member, channel] = tri[r : r + height, c : c + width]
            return carry

        lax.fori_loop(0, depth, multiply, 0)
        each(
            t_flips, lambda flip, off: outward(q, flip, off, slots(t_flips, 0), mine).start()
        )
        local_out(q).start()
        if q + ready < chunks:
            start_in(q + ready)
    for q in range(chunks):
        for which in range(2):
            source, landing, send, recv, flips = operands[which]
            each(
                flips,
                lambda flip, off: inward(
                    source, landing, send, recv, flips, q, flip, off, slots(flips, 0), mine
                ).wait_send(),
            )
        each(
            t_flips, lambda flip, off: outward(q, flip, off, slots(t_flips, 0), mine).wait_send()
        )
        each(
            t_flips,
            lambda flip, off: outward(q, flip, off, slots(t_flips, flip), behind(off)).wait_recv(),
        )
        local_out(q).wait()


def triangle(a, b, rows, cols, outgoing):
    hidden, height, width = a.shape
    half_cols = cols // 2
    members = rows * half_cols
    owned = hidden // members
    chunks = min(CHUNKS, owned)
    depth = owned // chunks
    n = rows * height
    a_flips, t_flips = (1, 2) if outgoing else (2, 1)

    def blocks(flips):
        return pltpu.VMEM((chunks, flips, members, depth, height, width), jnp.bfloat16)

    def sems(flips):
        return pltpu.SemaphoreType.DMA((chunks, flips, members))

    anywhere = pl.BlockSpec(memory_space=pl.ANY)
    return pl.pallas_call(
        functools.partial(triangle_kernel, outgoing, chunks, rows, half_cols),
        in_specs=[anywhere, anywhere],
        out_specs=anywhere,
        out_shape=jax.ShapeDtypeStruct((t_flips, hidden, height, width), jnp.bfloat16),
        scratch_shapes=[
            blocks(a_flips),
            blocks(1),
            blocks(t_flips),
            pltpu.VMEM((n, a_flips * half_cols * width), jnp.bfloat16),
            pltpu.VMEM((n, half_cols * width), jnp.bfloat16),
            sems(a_flips),
            sems(a_flips),
            sems(1),
            sems(1),
            sems(t_flips),
            sems(t_flips),
            pltpu.SemaphoreType.DMA((3, chunks)),
        ],
        compiler_params=pltpu.CompilerParams(
            collective_id=0 if outgoing else 1,
            has_side_effects=True,
            vmem_limit_bytes=48 * 2**20,
        ),
    )(a, b)


def update(field, pmask, w_inputs, w_gating, w_final, outgoing):
    rows, cols = lax.axis_size("row"), lax.axis_size("col")
    hidden = w_inputs.shape[1] // 4
    normed = layer_norm(field.astype(jnp.float32)).astype(jnp.bfloat16)

    def side(first):
        def one(start):
            w = w_inputs[:, start : start + hidden]
            return lax.dot_general(
                w, normed, (((0,), (2,)), ((), ())), preferred_element_type=jnp.float32
            )

        value = pmask[None] * jax.nn.sigmoid(one(first)) * one(first + hidden)
        return value.astype(jnp.bfloat16)

    a = side(0)
    b = side(2 * hidden)
    gate = jax.nn.sigmoid(jnp.dot(normed, w_gating, preferred_element_type=jnp.float32))
    tri = jnp.sum(triangle(a, b, rows, cols, outgoing).astype(jnp.float32), 0)
    tnorm = layer_norm(tri, 0).astype(jnp.bfloat16)
    value = lax.dot_general(
        tnorm, w_final, (((0,), (0,)), ((), ())), preferred_element_type=jnp.float32
    )
    return (field.astype(jnp.float32) + gate * value).astype(jnp.bfloat16)


def local(
    pair, token_mask, token_count, out_inputs, out_gating, out_final, in_inputs, in_gating, in_final
):
    height, width = pair.shape[:2]
    positions = lax.iota(jnp.int32, token_mask.shape[0])
    valid = (token_mask * (positions < token_count[0]).astype(jnp.int32)).astype(jnp.float32)
    row_valid = lax.dynamic_slice_in_dim(valid, lax.axis_index("row") * height, height)
    col_valid = lax.dynamic_slice_in_dim(valid, lax.axis_index("col") * width, width)
    pmask = row_valid[:, None] * col_valid[None, :]
    middle = update(pair, pmask, out_inputs, out_gating, out_final, True)
    return update(middle, pmask, in_inputs, in_gating, in_final, False)


def solution(mesh):
    tile = P(("groups", "row"), "col", None)
    in_specs = (tile, P("groups"), P("groups")) + (P(),) * 6
    return jax.shard_map(local, mesh=mesh, in_specs=in_specs, out_specs=tile, check_vma=False)
```

time: 684 us -> 783 us (1.14)
  Pallas kernels: 15.1 us -> 473 us
  blocking collectives: 392 us -> 0 us
  waiting for transfers between devices: 165 us -> 0 us
  local copies, waits for them, and re-layouts: 31.6 us -> 123 us
  other arithmetic: 16 us -> 99.5 us
  matrix products: 42.3 us -> 76 us
  starting transfers between devices: 12.2 us -> 0 us
    pallas_call x2, Pallas kernels: 15.1 us -> 473 us  [triangle(): pl.pallas_call(functools.partial(triangle_kernel, outgoing, chunks, rows,...]
    all_to_all x4 -> x0, blocking collectives: 392 us -> none  [exchange(): return lax.all_to_all(x, AXES, 0, 0, tiled=True)]
    all_to_all x2 -> x0, waiting for transfers between devices: 165 us -> none  [exchange(): return lax.all_to_all(x, AXES, 0, 0, tiled=True)]
    dot_general x0 -> x10, local copies, waits for them, and re-layouts: none -> 92.9 us  [the longest x8 74.3 us: one(): lax.dot_general(w, normed, (((0,), (2,)), ((), ())), preferred_element_ty...]
    convert_element_type x0 -> x5, other arithmetic: none -> 49.5 us  [the longest x2 32.1 us: side(): return value.astype(jnp.bfloat16)]
    reduce_sum x3 -> x4, other arithmetic: 4.69 us -> 36.5 us  [layer_norm(): mean = jnp.mean(x, axis=axis, keepdims=True)]
    dot_general x8, matrix products: 26.5 us -> 53 us  [one(): lax.dot_general(w, normed, (((0,), (2,)), ((), ())), preferred_element_ty...]
    all_to_all x2 -> x0, starting transfers between devices: 12.2 us -> none  [exchange(): return lax.all_to_all(x, AXES, 0, 0, tiled=True)]
  transfers between devices with their start and end apart: 2 -> 0, of which waited for: 2 -> 0; matrix products, arithmetic and copies ran while one was open for 4% -> 0% of each run, Pallas kernels for 0% -> 0%
where the time goes in v2:
time: 783 us; the launch traced here: 774 us
  Pallas kernels  473 us (60%)
  local copies, waits for them, and re-layouts  123 us (16%)
  other arithmetic  99.5 us (13%)
  matrix products  76 us (10%)
    pallas_call x2, Pallas kernels, triangle(): pl.pallas_call(functools.partial(triangle_kernel, outgoing, chunks, rows,...  473 us
    dot_general x8, local copies, waits for them, and re-layouts, one(): lax.dot_general(w, normed, (((0,), (2,)), ((), ())), preferred_element_ty...  74.3 us
    dot_general x8, matrix products, one(): lax.dot_general(w, normed, (((0,), (2,)), ((), ())), preferred_element_ty...  53 us
    reduce_sum x4, other arithmetic, layer_norm(): mean = jnp.mean(x, axis=axis, keepdims=True)  36.5 us
    convert_element_type x2, other arithmetic, side(): return value.astype(jnp.bfloat16)  32.1 us

profile of v2, /device:TPU:0, one launch (start us, length us, event | category | flops | bytes accessed | tf_op | source)
XLA Modules:
  0.0 773.7 jit_solution(11698865860347819270)
XLA Ops:
  1.5 6.7 copy.37
  17.9 6.9 copy.38
  24.8 6.6 fusion.38
  31.4 9.3 %copy.48 = f32[128,128,128]{1,0,2:T(8,128)} copy(f32[128,128,128]{2,1,0:T(8,128)} %fusion.38) | data formatting | bytes 16777216 | tf_op jit(solution)/shard_map/dot_general | solution.py:244
  40.7 6.6 fusion.40
  47.3 9.3 %copy.46 = f32[128,128,128]{1,0,2:T(8,128)} copy(f32[128,128,128]{2,1,0:T(8,128)} %fusion.40) | data formatting | bytes 16777216 | tf_op jit(solution)/shard_map/dot_general | solution.py:244
  56.6 6.6 fusion.42
  63.2 9.3 %copy.44 = f32[128,128,128]{1,0,2:T(8,128)} copy(f32[128,128,128]{2,1,0:T(8,128)} %fusion.42) | data formatting | bytes 16777216 | tf_op jit(solution)/shard_map/dot_general | solution.py:244
  72.5 6.6 fusion.44
  79.1 9.3 %copy.42 = f32[128,128,128]{1,0,2:T(8,128)} copy(f32[128,128,128]{2,1,0:T(8,128)} %fusion.44) | data formatting | bytes 16777216 | tf_op jit(solution)/shard_map/dot_general | solution.py:244
  88.4 15.5 %fusion.23 = (bf16[128,128,128]{2,1,0:T(8,128)(2,1)}, bf16[128,128,128]{2,1,0:T(8,128)(2,1)S(1)}) fusion(f32[128,128,128]{1,0,2:T(8,128)} %copy.48, f32[128,128,128]{1,0,2:T(8,128)} %copy.46, f32[128,128]{1,0:T(8,128)S(1)} %broadcast_multiply_fusion, f32[128,128,128]{1,0,2:T(8,128)} %copy.44, f32[128,128,128]{1,0,2:T(8,128)} %copy.42), kind=kLoop, calls=%fused_computation.41 | loop fusion | flops 25165824 | bytes 42008576 | tf_op jit(solution)/shard_map/convert_element_type | solution.py:249
  103.9 238.7 %shard_map.91 = bf16[2,128,128,128]{3,2,1,0:T(8,128)(2,1)} custom-call(bf16[128,128,128]{2,1,0:T(8,128)(2,1)S(1)} %get-tuple-element.12.a_hbm, bf16[128,128,128]{2,1,0:T(8,128)(2,1)} %get-tuple-element.11.b_hbm), custom_call_target="tpu_custom_call" | custom-call | tf_op jit(solution)/shard_map/pallas_call | solution.py:209
  342.6 11.2 %convert_reduce_fusion = (f32[128,128]{1,0:T(8,128)S(1)}, f32[128,128,128]{2,1,0:T(8,128)}) fusion(bf16[2,128,128,128]{3,2,1,0:T(8,128)(2,1)} %shard_map.91), kind=kLoop, calls=%fused_computation | loop fusion | flops 10469376 | bytes 16842752 | tf_op jit(solution)/shard_map/reduce_sum | solution.py:14
  353.8 4.4 multiply_reduce_fusion
  366.3 21.7 %convert_reduce_fusion.2 = (f32[128,128]{1,0:T(8,128)S(1)}, bf16[128,128,128]{1,0,2:T(8,128)(2,1)S(1)}) fusion(f32[128,128,128]{1,2,0:T(8,128)S(1)} %fusion.20, f32[128,128,128]{1,2,0:T(8,128)S(1)} %fusion.46, bf16[128,128,128]{1,0,2:T(8,128)(2,1)S(1)} %copy-done.4), kind=kLoop, calls=%fused_computation.4 | loop fusion | flops 18857984 | bytes 25231360 | tf_op jit(solution)/shard_map/reduce_sum | solution.py:14
  393.8 6.9 copy.52
  400.7 6.6 fusion.27
  407.3 9.3 %copy.61 = f32[128,128,128]{1,0,2:T(8,128)} copy(f32[128,128,128]{2,1,0:T(8,128)} %fusion.27) | data formatting | bytes 16777216 | tf_op jit(solution)/shard_map/dot_general | solution.py:244
  416.6 6.6 fusion.29
  423.3 9.3 %copy.59 = f32[128,128,128]{1,0,2:T(8,128)} copy(f32[128,128,128]{2,1,0:T(8,128)} %fusion.29) | data formatting | bytes 16777216 | tf_op jit(solution)/shard_map/dot_general | solution.py:244
  432.5 6.6 fusion.31
  439.2 9.3 %copy.57 = f32[128,128,128]{1,0,2:T(8,128)} copy(f32[128,128,128]{2,1,0:T(8,128)} %fusion.31) | data formatting | bytes 16777216 | tf_op jit(solution)/shard_map/dot_general | solution.py:244
  448.4 6.6 fusion.33
  455.1 9.3 %copy.55 = f32[128,128,128]{1,0,2:T(8,128)} copy(f32[128,128,128]{2,1,0:T(8,128)} %fusion.33) | data formatting | bytes 16777216 | tf_op jit(solution)/shard_map/dot_general | solution.py:244
  464.4 16.6 %fusion.25 = (bf16[128,128,128]{2,1,0:T(8,128)(2,1)}, bf16[128,128,128]{2,1,0:T(8,128)(2,1)}) fusion(f32[128,128,128]{1,0,2:T(8,128)} %copy.61, f32[128,128,128]{1,0,2:T(8,128)} %copy.59, f32[128,128]{1,0:T(8,128)S(1)} %broadcast_multiply_fusion, f32[128,128,128]{1,0,2:T(8,128)} %copy.57, f32[128,128,128]{1,0,2:T(8,128)} %copy.55), kind=kLoop, calls=%fused_computation.43 | loop fusion | flops 25165824 | bytes 42008576 | tf_op jit(solution)/shard_map/convert_element_type | solution.py:249
  481.0 234.8 %shard_map.92 = bf16[1,128,128,128]{3,2,1,0:T(8,128)(2,1)S(1)} custom-call(bf16[128,128,128]{2,1,0:T(8,128)(2,1)} %get-tuple-element.10.a_hbm, bf16[128,128,128]{2,1,0:T(8,128)(2,1)} %get-tuple-element.9.b_hbm), custom_call_target="tpu_custom_call" | custom-call | tf_op jit(solution)/shard_map/pallas_call | solution.py:209
  718.9 11.8 %fusion.18 = f32[128,128,128]{2,1,0:T(8,128)} fusion(bf16[128,128,128]{2,1,0:T(8,128)(2,1)S(1)} %fusion.12, bf16[128,128]{1,0:T(8,128)(2,1)S(1)} %copy-done.10), kind=kOutput, calls=%fused_computation.36 | convolution fusion | flops 536870912 | bytes 12615680 | tf_op jit(solution)/shard_map/dot_general | solution.py:256
  730.8 9.3 %copy.63 = f32[128,128,128]{1,0,2:T(8,128)} copy(f32[128,128,128]{2,1,0:T(8,128)} %fusion.18) | data formatting | bytes 16777216 | tf_op jit(solution)/shard_map/dot_general | solution.py:256
  740.1 6.6 fusion.35
  746.7 9.3 %copy.53 = f32[128,128,128]{1,0,2:T(8,128)} copy(f32[128,128,128]{2,1,0:T(8,128)} %fusion.35) | data formatting | bytes 16777216 | tf_op jit(solution)/shard_map/dot_general | solution.py:253
  756.0 10.4 %fusion.14 = bf16[128,128,128]{1,0,2:T(8,128)(2,1)} fusion(bf16[128,128,128]{1,0,2:T(8,128)(2,1)} %copy-done.6, f32[128,128,128]{1,0,2:T(8,128)} %copy.63, f32[128,128,128]{1,0,2:T(8,128)} %copy.53), kind=kLoop, calls=%fused_computation.24 | loop fusion | flops 14680064 | bytes 25165824 | tf_op jit(solution)/shard_map/convert_element_type | solution.py:259
  766.3 6.9 copy.64
  (46 shorter events, 27.4 us)
Async XLA Ops:
  0.0 360.9 %copy-start = (bf16[128,128]{1,0:T(8,128)(2,1)S(1)}, bf16[128,128]{1,0:T(8,128)(2,1)}, u32[]{:S(2)}) copy-start(bf16[128,128]{1,0:T(8,128)(2,1)} %param.14) | copy-start | bytes 98308
  8.3 6.3 copy-start.3
  14.6 10.2 %copy-start.7 = (bf16[128,512]{1,0:T(8,128)(2,1)S(1)}, bf16[128,512]{1,0:T(8,128)(2,1)}, u32[]{:S(2)}) copy-start(bf16[128,512]{1,0:T(8,128)(2,1)} %param.12) | copy-start | bytes 393220
  353.8 5.8 copy-start.5
  360.9 3.2 copy-start.2
  360.9 3.2 copy-start.9
  364.1 2.2 copy-start.4
  388.0 2.0 copy-start.6
  390.0 10.7 %copy-start.8 = (bf16[128,512]{1,0:T(8,128)(2,1)S(1)}, bf16[128,512]{1,0:T(8,128)(2,1)}, u32[]{:S(2)}) copy-start(bf16[128,512]{1,0:T(8,128)(2,1)} %param.15) | copy-start | bytes 393220
  715.8 3.2 copy-start.10
  730.8 9.3 %copy-start.11 = (bf16[128,128]{1,0:T(8,128)(2,1)S(1)}, bf16[128,128]{1,0:T(8,128)(2,1)}, u32[]{:S(2)}) copy-start(bf16[128,128]{1,0:T(8,128)(2,1)} %param.16) | copy-start | bytes 98308
  756.0 17.3 %copy-start.1 = (bf16[128,128]{1,0:T(8,128)(2,1)S(1)}, bf16[128,128]{1,0:T(8,128)(2,1)}, u32[]{:S(2)}) copy-start(bf16[128,128]{1,0:T(8,128)(2,1)} %param.14) | copy-start | bytes 98308

commit v3 on v2

--- a/solution.py
+++ b/solution.py
@@ -8,13 +8,6 @@
 from jax.sharding import PartitionSpec as P
 
 CHUNKS = 4
-
-
-def layer_norm(x, axis=-1):
-    mean = jnp.mean(x, axis=axis, keepdims=True)
-    centred = x - mean
-    var = jnp.mean(centred * centred, axis=axis, keepdims=True)
-    return centred * lax.rsqrt(var + 1e-05)
 
 
 MESH = pl.DeviceIdType.MESH
@@ -233,43 +226,134 @@
     )(a, b)
 
 
-def update(field, pmask, w_inputs, w_gating, w_final, outgoing):
-    rows, cols = lax.axis_size("row"), lax.axis_size("col")
-    hidden = w_inputs.shape[1] // 4
-    normed = layer_norm(field.astype(jnp.float32)).astype(jnp.bfloat16)
-
-    def side(first):
-        def one(start):
-            w = w_inputs[:, start : start + hidden]
-            return lax.dot_general(
-                w, normed, (((0,), (2,)), ((), ())), preferred_element_type=jnp.float32
-            )
-
-        value = pmask[None] * jax.nn.sigmoid(one(first)) * one(first + hidden)
-        return value.astype(jnp.bfloat16)
-
-    a = side(0)
-    b = side(2 * hidden)
-    gate = jax.nn.sigmoid(jnp.dot(normed, w_gating, preferred_element_type=jnp.float32))
-    tri = jnp.sum(triangle(a, b, rows, cols, outgoing).astype(jnp.float32), 0)
-    tnorm = layer_norm(tri, 0).astype(jnp.bfloat16)
-    value = lax.dot_general(
-        tnorm, w_final, (((0,), (0,)), ((), ())), preferred_element_type=jnp.float32
-    )
-    return (field.astype(jnp.float32) + gate * value).astype(jnp.bfloat16)
+def layer_norm(x, axis):
+    mean = jnp.mean(x, axis=axis, keepdims=True)
+    centred = x - mean
+    var = jnp.mean(centred * centred, axis=axis, keepdims=True)
+    return centred * lax.rsqrt(var + 1e-05)
+
+
+def sigmoid(x):
+    return 0.5 * jnp.tanh(0.5 * x) + 0.5
+
+
+def point_kernel(finishes, prepares, *refs):
+    refs = list(refs)
+    field_ref = refs.pop(0)
+    height, width, channels = field_ref.shape
+    if finishes:
+        tri_ref, gate_ref, final_ref = refs.pop(0), refs.pop(0), refs.pop(0)
+    if prepares:
+        mask_ref, inputs_ref, gating_ref = refs.pop(0), refs.pop(0), refs.pop(0)
+    if finishes:
+        middle_ref = refs.pop(0)
+    if prepares:
+        a_ref, b_ref, new_gate_ref = refs.pop(0), refs.pop(0), refs.pop(0)
+    one, two = refs
+
+    if finishes:
+        hidden = tri_ref.shape[1]
+        tri = jnp.sum(tri_ref[...].astype(jnp.float32), 0)
+        tnorm = layer_norm(tri, 0)
+        for h in range(hidden):
+            one[pl.ds(h, height, stride=hidden), :] = tnorm[h]
+
+    def line(i, carry):
+        field = field_ref[i].astype(jnp.float32)
+        if finishes:
+            at = pl.ds(pl.multiple_of(i * hidden, hidden), hidden)
+            value = lax.dot_general(
+                one[at, :].astype(jnp.bfloat16),
+                final_ref[...],
+                (((0,), (0,)), ((), ())),
+                preferred_element_type=jnp.float32,
+            )
+            rounded = (field + gate_ref[i] * value).astype(jnp.bfloat16)
+            middle_ref[i] = rounded
+            field = rounded.astype(jnp.float32)
+        if prepares:
+            size = inputs_ref.shape[0] // 4
+            normed = layer_norm(field, -1).astype(jnp.bfloat16)
+            proj = lax.dot_general(
+                inputs_ref[...], normed, (((1,), (1,)), ((), ())),
+                preferred_element_type=jnp.float32,
+            )
+            mask = mask_ref[pl.ds(i, 1), :]
+            at = pl.ds(pl.multiple_of(i * size, size), size)
+            one[at, :] = mask * sigmoid(proj[:size]) * proj[size : 2 * size]
+            two[at, :] = mask * sigmoid(proj[2 * size : 3 * size]) * proj[3 * size :]
+            new_gate_ref[i] = sigmoid(
+                jnp.dot(normed, gating_ref[...], preferred_element_type=jnp.float32)
+            )
+        return carry
+
+    lax.fori_loop(0, height, line, 0, unroll=4)
+    if prepares:
+        hidden = a_ref.shape[0]
+        for h in range(hidden):
+            rows = pl.ds(h, height, stride=hidden)
+            a_ref[h] = one[rows, :].astype(jnp.bfloat16)
+            b_ref[h] = two[rows, :].astype(jnp.bfloat16)
+
+
+def point(field, finish=None, prepare=None):
+    rows, width, channels = field.shape
+    block = 16
+    line_spec = pl.BlockSpec((block, width, channels), lambda i: (i, 0, 0))
+    args, in_specs, outs, out_specs = [field], [line_spec], [], []
+
+    def whole(array):
+        args.append(array)
+        in_specs.append(pl.BlockSpec(array.shape, lambda i: (0,) * array.ndim))
+
+    if finish is not None:
+        tri, gate, final = finish
+        hidden = tri.shape[1]
+        args.extend((tri, gate))
+        in_specs.append(
+            pl.BlockSpec((tri.shape[0], hidden, block, width), lambda i: (0, 0, i, 0))
+        )
+        in_specs.append(line_spec)
+        whole(final)
+        outs.append(jax.ShapeDtypeStruct(field.shape, jnp.bfloat16))
+        out_specs.append(line_spec)
+    if prepare is not None:
+        mask, inputs, gating = prepare
+        hidden = inputs.shape[1] // 4
+        args.append(mask)
+        in_specs.append(pl.BlockSpec((block, width), lambda i: (i, 0)))
+        whole(inputs.T)
+        whole(gating)
+        outs.extend([jax.ShapeDtypeStruct((hidden, rows, width), jnp.bfloat16)] * 2)
+        out_specs.extend([pl.BlockSpec((hidden, block, width), lambda i: (0, i, 0))] * 2)
+        outs.append(jax.ShapeDtypeStruct(field.shape, jnp.float32))
+        out_specs.append(line_spec)
+    return pl.pallas_call(
+        functools.partial(point_kernel, finish is not None, prepare is not None),
+        grid=(rows // block,),
+        in_specs=in_specs,
+        out_specs=out_specs,
+        out_shape=outs,
+        scratch_shapes=[pltpu.VMEM((block * hidden, width), jnp.float32)] * 2,
+        compiler_params=pltpu.CompilerParams(vmem_limit_bytes=40 * 2**20),
+    )(*args)
 
 
 def local(
     pair, token_mask, token_count, out_inputs, out_gating, out_final, in_inputs, in_gating, in_final
 ):
     height, width = pair.shape[:2]
+    sizes = lax.axis_size("row"), lax.axis_size("col")
     positions = lax.iota(jnp.int32, token_mask.shape[0])
     valid = (token_mask * (positions < token_count[0]).astype(jnp.int32)).astype(jnp.float32)
     row_valid = lax.dynamic_slice_in_dim(valid, lax.axis_index("row") * height, height)
     col_valid = lax.dynamic_slice_in_dim(valid, lax.axis_index("col") * width, width)
     pmask = row_valid[:, None] * col_valid[None, :]
-    middle = update(pair, pmask, out_inputs, out_gating, out_final, True)
-    return update(middle, pmask, in_inputs, in_gating, in_final, False)
+    a, b, gate = point(pair, prepare=(pmask, out_inputs, out_gating))
+    tri = triangle(a, b, *sizes, True)
+    middle, a, b, gate = point(pair, (tri, gate, out_final), (pmask, in_inputs, in_gating))
+    tri = triangle(a, b, *sizes, False)
+    return point(middle, finish=(tri, gate, in_final))[0]
 
 
 def solution(mesh):

time: 783 us -> 604 us (0.77); the launches traced: 774 us -> 604 us
  Pallas kernels: 473 us -> 591 us
  local copies, waits for them, and re-layouts: 123 us -> 11.1 us
  other arithmetic: 99.5 us -> 0.77 us
  matrix products: 76 us -> 0 us
    pallas_call x0 -> x3, Pallas kernels: none -> 118 us  [point(): pl.pallas_call(functools.partial(point_kernel, finish is not None, prepar...]
    dot_general x10 -> x0, local copies, waits for them, and re-layouts: 92.9 us -> none  [the longest x8 74.3 us: one(): lax.dot_general(w, normed, (((0,), (2,)), ((), ())), preferred_element_ty...]
    dot_general x12 -> x0, matrix products: 76 us -> none  [the longest x8 53 us: one(): lax.dot_general(w, normed, (((0,), (2,)), ((), ())), preferred_element_ty...]
    convert_element_type x7 -> x0, other arithmetic: 52.1 us -> none  [the longest x2 32.1 us: side(): return value.astype(jnp.bfloat16)]
    reduce_sum x8 -> x0, other arithmetic: 46.6 us -> none  [the longest x4 36.5 us: layer_norm(): mean = jnp.mean(x, axis=axis, keepdims=True)]
    convert_element_type x3 -> x0, local copies, waits for them, and re-layouts: 20.6 us -> none  [the longest x2 13.8 us: update(): normed = layer_norm(field.astype(jnp.float32)).astype(jnp.bfloat16)]
where the time goes in v3:
time: 604 us
  Pallas kernels  591 us (98%)
  local copies, waits for them, and re-layouts  11.1 us (2%)
    pallas_call x2, Pallas kernels, triangle(): pl.pallas_call(functools.partial(triangle_kernel, outgoing, chunks, rows,...  473 us
    pallas_call x3, Pallas kernels, point(): pl.pallas_call(functools.partial(point_kernel, finish is not None, prepar...  118 us

profile of v3, /device:TPU:0, one launch (start us, length us, event | category | flops | bytes accessed | tf_op | source)
XLA Modules:
  0.0 603.5 jit_solution(14904443295745144649)
XLA Ops:
  0.7 0.7 select_convert_fusion
  1.3 0.1 fusion
  1.4 0.1 broadcast_multiply_fusion.refs_1_.refs_4_
  1.5 1.0 copy.10
  2.5 1.0 copy.11
  3.6 0.0 copy-start
  3.6 2.2 copy-done
  5.8 0.0 copy-start.4
  5.8 0.8 copy-done.4
  6.5 31.2 %shard_map.91 = (bf16[128,128,128]{2,1,0:T(8,128)(2,1)S(1)}, bf16[128,128,128]{2,1,0:T(8,128)(2,1)S(1)}, f32[128,128,128]{2,1,0:T(8,128)}) custom-call(bf16[128,128,128]{2,1,0:T(8,128)(2,1)S(1)} %copy-done, f32[128,128]{1,0:T(8,128)S(1)} %broadcast_multiply_fusion.refs_1_.refs_4_, bf16[512,128]{1,0:T(8,128)(2,1)S(1)} %bitcast.4, bf16[128,128]{1,0:T(8,128)(2,1)S(1)} %copy-done.4), custom_call_target="tpu_custom_call" | custom-call | tf_op jit(solution)/shard_map/pallas_call | solution.py:331
  37.7 0.0 copy-start.3
  37.7 2.0 copy-done.3
  39.7 0.0 copy-start.5
  39.7 0.0 copy-start.6
  39.7 238.7 %shard_map.92.refs_1_ = bf16[2,128,128,128]{3,2,1,0:T(8,128)(2,1)} custom-call(bf16[128,128,128]{2,1,0:T(8,128)(2,1)S(1)} %get-tuple-element.12.a_hbm, bf16[128,128,128]{2,1,0:T(8,128)(2,1)} %copy-done.3), custom_call_target="tpu_custom_call" | custom-call | tf_op jit(solution)/shard_map/pallas_call | solution.py:202
  278.4 0.0 copy-done.5
  278.4 0.0 copy-done.6
  278.4 69.2 %shard_map.93 = (bf16[128,128,128]{2,1,0:T(8,128)(2,1)S(1)}, bf16[128,128,128]{2,1,0:T(8,128)(2,1)S(1)}, bf16[128,128,128]{2,1,0:T(8,128)(2,1)S(1)}, f32[128,128,128]{2,1,0:T(8,128)}) custom-call(bf16[128,128,128]{2,1,0:T(8,128)(2,1)} %refs_0_.3, bf16[2,128,128,128]{3,2,1,0:T(8,128)(2,1)} %shard_map.92.refs_1_, f32[128,128,128]{2,1,0:T(8,128)} %get-tuple-element.14.refs_2_, ...), custom_call_target="tpu_custom_call" | custom-call | tf_op jit(solution)/shard_map/pallas_call | solution.py:331
  347.7 0.0 copy-start.1
  347.7 2.0 copy-done.1
  349.7 0.0 copy-start.2
  349.7 2.0 copy-done.2
  351.7 0.0 copy-start.7
  351.7 234.5 %shard_map.94.refs_1_ = bf16[1,128,128,128]{3,2,1,0:T(8,128)(2,1)S(1)} custom-call(bf16[128,128,128]{2,1,0:T(8,128)(2,1)} %copy-done.1, bf16[128,128,128]{2,1,0:T(8,128)(2,1)} %copy-done.2), custom_call_target="tpu_custom_call" | custom-call | tf_op jit(solution)/shard_map/pallas_call | solution.py:202
  586.2 0.0 copy-done.7
  586.2 17.3 %shard_map.95 = bf16[128,128,128]{2,1,0:T(8,128)(2,1)} custom-call(bf16[128,128,128]{2,1,0:T(8,128)(2,1)S(1)} %get-tuple-element.15.refs_0_, bf16[1,128,128,128]{3,2,1,0:T(8,128)(2,1)S(1)} %shard_map.94.refs_1_, f32[128,128,128]{2,1,0:T(8,128)} %get-tuple-element.18.refs_2_, bf16[128,128]{1,0:T(8,128)(2,1)S(1)} %copy-done.7), custom_call_target="tpu_custom_call" | custom-call | tf_op jit(solution)/shard_map/pallas_call | solution.py:331
Async XLA Ops:
  3.6 2.2 copy-start
  5.8 0.8 copy-start.4
  37.7 2.0 copy-start.3
  39.7 238.7 %copy-start.5 = (bf16[128,128]{1,0:T(8,128)(2,1)S(1)}, bf16[128,128]{1,0:T(8,128)(2,1)}, u32[]{:S(2)}) copy-start(bf16[128,128]{1,0:T(8,128)(2,1)} %refs_3_.4) | copy-start | bytes 98308
  39.7 238.7 %copy-start.6 = (bf16[128,128]{1,0:T(8,128)(2,1)S(1)}, bf16[128,128]{1,0:T(8,128)(2,1)}, u32[]{:S(2)}) copy-start(bf16[128,128]{1,0:T(8,128)(2,1)} %refs_6_.1) | copy-start | bytes 98308
  347.7 2.0 copy-start.1
  349.7 2.0 copy-start.2
  351.7 234.5 %copy-start.7 = (bf16[128,128]{1,0:T(8,128)(2,1)S(1)}, bf16[128,128]{1,0:T(8,128)(2,1)}, u32[]{:S(2)}) copy-start(bf16[128,128]{1,0:T(8,128)(2,1)} %refs_3_.5) | copy-start | bytes 98308

commit v4 on v3

--- a/solution.py
+++ b/solution.py
@@ -253,17 +253,18 @@
 
     if finishes:
         hidden = tri_ref.shape[1]
-        tri = jnp.sum(tri_ref[...].astype(jnp.float32), 0)
-        tnorm = layer_norm(tri, 0)
         for h in range(hidden):
-            one[pl.ds(h, height, stride=hidden), :] = tnorm[h]
-
-    def line(i, carry):
+            tri = tri_ref[0, h].astype(jnp.float32)
+            for side in range(1, tri_ref.shape[0]):
+                tri = tri + tri_ref[side, h].astype(jnp.float32)
+            one[pl.ds(h, height, stride=hidden), :] = tri
+
+    def line(i):
         field = field_ref[i].astype(jnp.float32)
         if finishes:
-            at = pl.ds(pl.multiple_of(i * hidden, hidden), hidden)
+            at = slice(i * hidden, (i + 1) * hidden)
             value = lax.dot_general(
-                one[at, :].astype(jnp.bfloat16),
+                layer_norm(one[at, :], 0).astype(jnp.bfloat16),
                 final_ref[...],
                 (((0,), (0,)), ((), ())),
                 preferred_element_type=jnp.float32,
@@ -278,16 +279,16 @@
                 inputs_ref[...], normed, (((1,), (1,)), ((), ())),
                 preferred_element_type=jnp.float32,
             )
-            mask = mask_ref[pl.ds(i, 1), :]
-            at = pl.ds(pl.multiple_of(i * size, size), size)
+            mask = mask_ref[i : i + 1, :]
+            at = slice(i * size, (i + 1) * size)
             one[at, :] = mask * sigmoid(proj[:size]) * proj[size : 2 * size]
             two[at, :] = mask * sigmoid(proj[2 * size : 3 * size]) * proj[3 * size :]
             new_gate_ref[i] = sigmoid(
                 jnp.dot(normed, gating_ref[...], preferred_element_type=jnp.float32)
             )
-        return carry
-
-    lax.fori_loop(0, height, line, 0, unroll=4)
+
+    for i in range(height):
+        line(i)
     if prepares:
         hidden = a_ref.shape[0]
         for h in range(hidden):

time: 604 us -> 590 us (0.977)
  Pallas kernels: 591 us -> 577 us
    pallas_call x3, Pallas kernels: 118 us -> 104 us  [point(): pl.pallas_call(functools.partial(point_kernel, finish is not None, prepar...]
where the time goes in v4:
time: 590 us
  Pallas kernels  577 us (98%)
  local copies, waits for them, and re-layouts  11.1 us (2%)
    pallas_call x2, Pallas kernels, triangle(): pl.pallas_call(functools.partial(triangle_kernel, outgoing, chunks, rows,...  473 us
    pallas_call x3, Pallas kernels, point(): pl.pallas_call(functools.partial(point_kernel, finish is not None, prepar...  104 us

profile of v4, /device:TPU:0, one launch (start us, length us, event | category | flops | bytes accessed | tf_op | source)
XLA Modules:
  0.0 589.9 jit_solution(7638133516153571784)
XLA Ops:
  0.7 0.7 select_convert_fusion
  1.3 0.1 fusion
  1.4 0.1 broadcast_multiply_fusion.refs_1_.refs_4_
  1.5 1.0 copy.10
  2.5 1.0 copy.11
  3.6 0.0 copy-start
  3.6 2.2 copy-done
  5.8 0.0 copy-start.4
  5.8 0.8 copy-done.4
  6.5 27.8 %shard_map.91 = (bf16[128,128,128]{2,1,0:T(8,128)(2,1)S(1)}, bf16[128,128,128]{2,1,0:T(8,128)(2,1)S(1)}, f32[128,128,128]{2,1,0:T(8,128)}) custom-call(bf16[128,128,128]{2,1,0:T(8,128)(2,1)S(1)} %copy-done, f32[128,128]{1,0:T(8,128)S(1)} %broadcast_multiply_fusion.refs_1_.refs_4_, bf16[512,128]{1,0:T(8,128)(2,1)S(1)} %bitcast.4, bf16[128,128]{1,0:T(8,128)(2,1)S(1)} %copy-done.4), custom_call_target="tpu_custom_call" | custom-call | tf_op jit(solution)/shard_map/pallas_call | solution.py:332
  34.3 0.0 copy-start.3
  34.4 2.0 copy-done.3
  36.4 0.0 copy-start.5
  36.4 0.0 copy-start.6
  36.4 238.7 %shard_map.92.refs_1_ = bf16[2,128,128,128]{3,2,1,0:T(8,128)(2,1)} custom-call(bf16[128,128,128]{2,1,0:T(8,128)(2,1)S(1)} %get-tuple-element.12.a_hbm, bf16[128,128,128]{2,1,0:T(8,128)(2,1)} %copy-done.3), custom_call_target="tpu_custom_call" | custom-call | tf_op jit(solution)/shard_map/pallas_call | solution.py:202
  275.1 0.0 copy-done.5
  275.1 0.0 copy-done.6
  275.1 64.4 %shard_map.93 = (bf16[128,128,128]{2,1,0:T(8,128)(2,1)S(1)}, bf16[128,128,128]{2,1,0:T(8,128)(2,1)S(1)}, bf16[128,128,128]{2,1,0:T(8,128)(2,1)S(1)}, f32[128,128,128]{2,1,0:T(8,128)}) custom-call(bf16[128,128,128]{2,1,0:T(8,128)(2,1)} %refs_0_.3, bf16[2,128,128,128]{3,2,1,0:T(8,128)(2,1)} %shard_map.92.refs_1_, f32[128,128,128]{2,1,0:T(8,128)} %get-tuple-element.14.refs_2_, ...), custom_call_target="tpu_custom_call" | custom-call | tf_op jit(solution)/shard_map/pallas_call | solution.py:332
  339.5 0.0 copy-start.1
  339.5 2.0 copy-done.1
  341.5 0.0 copy-start.2
  341.5 2.0 copy-done.2
  343.5 0.0 copy-start.7
  343.5 234.5 %shard_map.94.refs_1_ = bf16[1,128,128,128]{3,2,1,0:T(8,128)(2,1)S(1)} custom-call(bf16[128,128,128]{2,1,0:T(8,128)(2,1)} %copy-done.1, bf16[128,128,128]{2,1,0:T(8,128)(2,1)} %copy-done.2), custom_call_target="tpu_custom_call" | custom-call | tf_op jit(solution)/shard_map/pallas_call | solution.py:202
  578.0 0.0 copy-done.7
  578.0 11.9 %shard_map.95 = bf16[128,128,128]{2,1,0:T(8,128)(2,1)} custom-call(bf16[128,128,128]{2,1,0:T(8,128)(2,1)S(1)} %get-tuple-element.15.refs_0_, bf16[1,128,128,128]{3,2,1,0:T(8,128)(2,1)S(1)} %shard_map.94.refs_1_, f32[128,128,128]{2,1,0:T(8,128)} %get-tuple-element.18.refs_2_, bf16[128,128]{1,0:T(8,128)(2,1)S(1)} %copy-done.7), custom_call_target="tpu_custom_call" | custom-call | tf_op jit(solution)/shard_map/pallas_call | solution.py:332
Async XLA Ops:
  3.6 2.2 copy-start
  5.8 0.8 copy-start.4
  34.3 2.0 copy-start.3
  36.4 238.7 %copy-start.5 = (bf16[128,128]{1,0:T(8,128)(2,1)S(1)}, bf16[128,128]{1,0:T(8,128)(2,1)}, u32[]{:S(2)}) copy-start(bf16[128,128]{1,0:T(8,128)(2,1)} %refs_3_.4) | copy-start | bytes 98308
  36.4 238.7 %copy-start.6 = (bf16[128,128]{1,0:T(8,128)(2,1)S(1)}, bf16[128,128]{1,0:T(8,128)(2,1)}, u32[]{:S(2)}) copy-start(bf16[128,128]{1,0:T(8,128)(2,1)} %refs_6_.1) | copy-start | bytes 98308
  339.5 2.0 copy-start.1
  341.5 2.0 copy-start.2
  343.5 234.5 %copy-start.7 = (bf16[128,128]{1,0:T(8,128)(2,1)S(1)}, bf16[128,128]{1,0:T(8,128)(2,1)}, u32[]{:S(2)}) copy-start(bf16[128,128]{1,0:T(8,128)(2,1)} %refs_3_.5) | copy-start | bytes 98308

commit v5 on v4

--- a/solution.py
+++ b/solution.py
@@ -352,7 +352,8 @@
     pmask = row_valid[:, None] * col_valid[None, :]
     a, b, gate = point(pair, prepare=(pmask, out_inputs, out_gating))
     tri = triangle(a, b, *sizes, True)
-    middle, a, b, gate = point(pair, (tri, gate, out_final), (pmask, in_inputs, in_gating))
+    middle = point(pair, finish=(tri, gate, out_final))[0]
+    a, b, gate = point(middle, prepare=(pmask, in_inputs, in_gating))
     tri = triangle(a, b, *sizes, False)
     return point(middle, finish=(tri, gate, in_final))[0]
 

time: 590 us -> 570 us (0.966)
  Pallas kernels: 577 us -> 553 us
    pallas_call x3 -> x4, Pallas kernels: 104 us -> 79.8 us  [point(): pl.pallas_call(functools.partial(point_kernel, finish is not None, prepar...]
    unnamed x18 -> x28, local copies, waits for them, and re-layouts: 11 us -> 14.2 us
where the time goes in v5:
time: 570 us; the launch traced here: 569 us
  Pallas kernels  553 us (97%)
  local copies, waits for them, and re-layouts  14.3 us (3%)
    pallas_call x2, Pallas kernels, triangle(): pl.pallas_call(functools.partial(triangle_kernel, outgoing, chunks, rows,...  473 us
    pallas_call x4, Pallas kernels, point(): pl.pallas_call(functools.partial(point_kernel, finish is not None, prepar...  79.8 us
    unnamed x28, local copies, waits for them, and re-layouts  14.2 us

profile of v5, /device:TPU:0, one launch (start us, length us, event | category | flops | bytes accessed | tf_op | source)
XLA Modules:
  0.0 568.9 jit_solution(7905403766133668297)
XLA Ops:
  0.7 0.7 select_convert_fusion
  1.3 0.1 fusion
  1.4 0.1 broadcast_multiply_fusion.refs_1_
  1.5 1.0 copy.10
  2.5 0.0 copy-start.3
  2.5 2.2 copy-done.3
  4.7 0.0 copy-start.8
  4.7 0.8 copy-done.8
  5.5 27.9 %shard_map.91 = (bf16[128,128,128]{2,1,0:T(8,128)(2,1)S(1)}, bf16[128,128,128]{2,1,0:T(8,128)(2,1)S(1)}, f32[128,128,128]{2,1,0:T(8,128)}) custom-call(bf16[128,128,128]{2,1,0:T(8,128)(2,1)S(1)} %copy-done.3, f32[128,128]{1,0:T(8,128)S(1)} %broadcast_multiply_fusion.refs_1_, bf16[512,128]{1,0:T(8,128)(2,1)S(1)} %bitcast.5, bf16[128,128]{1,0:T(8,128)(2,1)S(1)} %copy-done.8), custom_call_target="tpu_custom_call" | custom-call | tf_op jit(solution)/shard_map/pallas_call | solution.py:332
  33.4 0.0 copy-start.7
  33.4 2.0 copy-done.7
  35.4 0.0 copy-start.4
  35.4 238.7 %shard_map.92.refs_1_ = bf16[2,128,128,128]{3,2,1,0:T(8,128)(2,1)} custom-call(bf16[128,128,128]{2,1,0:T(8,128)(2,1)S(1)} %get-tuple-element.11.a_hbm, bf16[128,128,128]{2,1,0:T(8,128)(2,1)} %copy-done.7), custom_call_target="tpu_custom_call" | custom-call | tf_op jit(solution)/shard_map/pallas_call | solution.py:202
  274.1 0.0 copy-done.4
  274.1 0.0 copy-done.9
  274.1 0.0 copy-start.12
  274.1 0.0 copy-start.10
  274.1 12.2 %shard_map.93.refs_0_ = bf16[128,128,128]{2,1,0:T(8,128)(2,1)S(1)} custom-call(bf16[128,128,128]{2,1,0:T(8,128)(2,1)S(1)} %copy-done.4, bf16[2,128,128,128]{3,2,1,0:T(8,128)(2,1)} %shard_map.92.refs_1_, f32[128,128,128]{2,1,0:T(8,128)} %get-tuple-element.13.refs_2_, bf16[128,128]{1,0:T(8,128)(2,1)S(1)} %copy-done.9), custom_call_target="tpu_custom_call" | custom-call | tf_op jit(solution)/shard_map/pallas_call | solution.py:332
  286.3 0.0 copy-start
  286.3 2.0 copy-done
  288.3 0.0 copy-done.12
  288.3 0.1 copy.11
  288.5 0.0 copy-done.10
  288.5 0.0 copy-start.1
  288.5 2.2 copy-done.1
  290.7 27.9 %shard_map.94 = (bf16[128,128,128]{2,1,0:T(8,128)(2,1)S(1)}, bf16[128,128,128]{2,1,0:T(8,128)(2,1)S(1)}, f32[128,128,128]{2,1,0:T(8,128)}) custom-call(bf16[128,128,128]{2,1,0:T(8,128)(2,1)S(1)} %copy-done.1, f32[128,128]{1,0:T(8,128)S(1)} %broadcast_multiply_fusion.refs_1_, bf16[512,128]{1,0:T(8,128)(2,1)S(1)} %bitcast.4, bf16[128,128]{1,0:T(8,128)(2,1)S(1)} %copy-done.10), custom_call_target="tpu_custom_call" | custom-call | tf_op jit(solution)/shard_map/pallas_call | solution.py:332
  318.5 2.0 copy-done.5
  320.5 1.9 copy-done.6
  322.4 234.6 %shard_map.95.refs_1_ = bf16[1,128,128,128]{3,2,1,0:T(8,128)(2,1)S(1)} custom-call(bf16[128,128,128]{2,1,0:T(8,128)(2,1)} %copy-done.5, bf16[128,128,128]{2,1,0:T(8,128)(2,1)} %copy-done.6), custom_call_target="tpu_custom_call" | custom-call | tf_op jit(solution)/shard_map/pallas_call | solution.py:202
  557.0 0.0 copy-done.2
  557.0 0.0 copy-done.11
  557.0 11.9 %shard_map.96 = bf16[128,128,128]{2,1,0:T(8,128)(2,1)} custom-call(bf16[128,128,128]{2,1,0:T(8,128)(2,1)S(1)} %copy-done.2, bf16[1,128,128,128]{3,2,1,0:T(8,128)(2,1)S(1)} %shard_map.95.refs_1_, f32[128,128,128]{2,1,0:T(8,128)} %get-tuple-element.16.refs_2_, bf16[128,128]{1,0:T(8,128)(2,1)S(1)} %copy-done.11), custom_call_target="tpu_custom_call" | custom-call | tf_op jit(solution)/shard_map/pallas_call | solution.py:332
  (5 shorter events, 0.0 us)
Async XLA Ops:
  2.5 2.2 copy-start.3
  4.7 0.8 copy-start.8
  33.4 2.0 copy-start.7
  35.4 238.7 %copy-start.4 = (bf16[128,128,128]{2,1,0:T(8,128)(2,1)S(1)}, bf16[128,128,128]{2,1,0:T(8,128)(2,1)}, u32[]{:S(2)}) copy-start(bf16[128,128,128]{2,1,0:T(8,128)(2,1)} %refs_0_.3) | copy-start | bytes 12582916
  35.4 238.7 %copy-start.9 = (bf16[128,128]{1,0:T(8,128)(2,1)S(1)}, bf16[128,128]{1,0:T(8,128)(2,1)}, u32[]{:S(2)}) copy-start(bf16[128,128]{1,0:T(8,128)(2,1)} %refs_3_.5) | copy-start | bytes 98308
  274.1 14.2 %copy-start.12 = (bf16[128,512]{1,0:T(8,128)(2,1)S(1)}, bf16[128,512]{1,0:T(8,128)(2,1)}, u32[]{:S(2)}) copy-start(bf16[128,512]{1,0:T(8,128)(2,1)} %param.15) | copy-start | bytes 393220
  274.1 14.3 %copy-start.10 = (bf16[128,128]{1,0:T(8,128)(2,1)S(1)}, bf16[128,128]{1,0:T(8,128)(2,1)}, u32[]{:S(2)}) copy-start(bf16[128,128]{1,0:T(8,128)(2,1)} %refs_3_.6) | copy-start | bytes 98308
  286.3 2.0 copy-start
  288.5 2.2 copy-start.1
  318.5 2.0 copy-start.5
  320.5 1.9 copy-start.6
  322.4 234.6 %copy-start.2 = (bf16[128,128,128]{2,1,0:T(8,128)(2,1)S(1)}, bf16[128,128,128]{2,1,0:T(8,128)(2,1)}, u32[]{:S(2)}) copy-start(bf16[128,128,128]{2,1,0:T(8,128)(2,1)} %copy-done) | copy-start | bytes 12582916
  322.4 234.6 %copy-start.11 = (bf16[128,128]{1,0:T(8,128)(2,1)S(1)}, bf16[128,128]{1,0:T(8,128)(2,1)}, u32[]{:S(2)}) copy-start(bf16[128,128]{1,0:T(8,128)(2,1)} %refs_3_.7) | copy-start | bytes 98308
